TPU v7x, 128 devices: a whole 4x4x4 slice. The times are simulated.
128 devices in a mesh: face: 8 (over z_lo, x), sub: 16 (over y, z_hi, core).
Axes of the slice: x: 4, y: 4, z: 4 (z_hi: 2, z_lo: 2; z = z_hi * 2 + z_lo), core: 2. Of those that a mesh axis runs over, the one named last changes fastest.
Arguments:
- tokens: bfloat16 [131072, 1024], P(('face', 'sub')), may hold values from -6 to 6
- w_qkv: bfloat16 [1024, 3072], replicated
- w_out: bfloat16 [1024, 1024], replicated, may hold values from -0.1875 to 0.1875
- neighbours: int32 [2048, 9], P(('face', 'sub')), may hold values from 0 to 2047, as said below
- parent_one: int32 [131072], P(('face', 'sub')), may hold values from 0 to 127, as said below
- parent_two: int32 [128], replicated, may hold values from 0 to 31, as said below
- level_bias: float32 [2, 16], replicated, may hold values from -2 to 0
Outputs:
- mixed: bfloat16 [131072, 1024], P(('face', 'sub'))
Inputs may be any that keep to these rules, and one draw needn't show every extreme that they name: Fine blocks lie on a periodic grid of 2 * 8 rows by 8 * 16 columns; block id = device * 16 + r * 8 + c, device = face index * 16 + sub index. Each row lists the block and its eight neighbours on that grid in row-major order, except that in some rows one diagonal neighbour is replaced by the block itself. `parent_one`: every token of a fine block has the same first-level cell, and the 16 blocks of each aligned 4 x 4 square of the block grid share one; each cell has 1024 tokens. `parent_two`: the four first-level cells of each aligned 2 x 2 square of cells share one second-level cell.
All inputs are finite; a program needn't handle non-finite values.
Results may differ from a plain program's by a relative error of at most 0.014.
Values may be sent and summed in bfloat16 or wider, within the bound.
A program may use at most 256 MiB of HBM per device.

v0:
```python
import jax
import jax.numpy as jnp
from jax import lax
from jax.sharding import PartitionSpec as P

HEADS = 16
HD = 64
BT = 64
BC = 8


def padded(block, sides, width):
    for axis, dim in sides:
        count = lax.axis_size(axis)
        forward = [(i, i + 1) for i in range(count - 1)]
        forward.append((count - 1, 0))
        backward = [(target, source) for source, target in forward]
        low = lax.ppermute(
            lax.slice_in_dim(block, block.shape[dim] - width, None, axis=dim), axis, forward
        )
        high = lax.ppermute(lax.slice_in_dim(block, 0, width, axis=dim), axis, backward)
        block = jnp.concatenate([low, block, high], axis=dim)
    return block


def normalize(sums):
    count = sums.shape[0]
    grouped = sums.reshape(count, 2, HEADS, HD)
    grouped = grouped * lax.rsqrt(jnp.mean(grouped * grouped, axis=-1, keepdims=True) + 1e-05)
    return grouped.reshape(count, 2 * HEADS * HD).astype(jnp.bfloat16)


def head_major(block_rows):
    count = block_rows.shape[0]
    return block_rows.reshape(count, BT, 2, HEADS, HD).transpose(0, 2, 3, 1, 4)


def body(tokens, w_qkv, w_out, neighbours, parent_one, parent_two, level_bias):
    width = tokens.shape[1]
    blocks = neighbours.shape[0]
    columns = BC
    row_count = blocks // columns
    proj = jnp.dot(tokens, w_qkv, preferred_element_type=jnp.float32).astype(jnp.bfloat16)
    query = proj[:, :width]
    pairs = proj[:, width:]
    grid = head_major(pairs.reshape(blocks, BT, 2 * width)).reshape(
        row_count, columns, 2, HEADS, BT, HD
    )
    extended = padded(grid, (("face", 0), ("sub", 1)), 1)
    ext_flat = extended.reshape(-1, 2, HEADS, BT, HD)
    face_count = lax.axis_size("face")
    sub_count = lax.axis_size("sub")
    my_face = lax.axis_index("face")
    my_sub = lax.axis_index("sub")
    owner = neighbours // blocks
    local = neighbours % blocks
    grow = owner // sub_count * row_count + local // columns
    gcol = owner % sub_count * columns + local % columns
    halo_r = (grow - my_face * row_count + 1) % (row_count * face_count)
    halo_c = (gcol - my_sub * columns + 1) % (columns * sub_count)
    flat = halo_r * (columns + 2) + halo_c
    coarse = parent_two.shape[0]
    upper_count = coarse // 4
    onehot_one = (parent_one[None, :] == jnp.arange(coarse, dtype=jnp.int32)[:, None]).astype(
        jnp.bfloat16
    )
    partial_value = jnp.dot(onehot_one, pairs, preferred_element_type=jnp.float32)
    sums_one = lax.psum(partial_value, ("face", "sub"))
    onehot_two = (parent_two[None, :] == jnp.arange(upper_count, dtype=jnp.int32)[:, None]).astype(
        jnp.float32
    )
    sums_two = jnp.dot(onehot_two, sums_one, precision=lax.Precision.HIGHEST)
    pooled_one = normalize(sums_one)
    pooled_two = normalize(sums_two)
    far = jnp.concatenate([pooled_one, pooled_two], axis=0)
    far_keys = far[:, :width].reshape(-1, HEADS, HD)
    far_vals = far[:, width:].reshape(-1, HEADS, HD)
    bias = jnp.concatenate(
        [
            jnp.broadcast_to(level_bias[0], (coarse, HEADS)),
            jnp.broadcast_to(level_bias[1], (upper_count, HEADS)),
        ],
        axis=0,
    ).T
    scale = HD ** (-0.5)
    q_groups = (
        query.reshape(blocks, BT, HEADS, HD)
        .transpose(0, 2, 1, 3)
        .reshape(blocks // 8, 8, HEADS, BT, HD)
    )
    idx_groups = flat.reshape(blocks // 8, 8, 9)

    def attend(args):
        qb, ib = args
        near = ext_flat[ib]
        s_near = (
            jnp.einsum("bhqd,bjhkd->bhqjk", qb, near[:, :, 0], preferred_element_type=jnp.float32)
            * scale
        )
        s_near = s_near.reshape(8, HEADS, BT, 9 * BT)
        s_far = (
            jnp.einsum("bhqd,khd->bhqk", qb, far_keys, preferred_element_type=jnp.float32) * scale
            + bias[None, :, None, :]
        )
        weights = jax.nn.softmax(jnp.concatenate([s_near, s_far], axis=-1), axis=-1).astype(
            jnp.bfloat16
        )
        w_near = weights[..., : 9 * BT].reshape(8, HEADS, BT, 9, BT)
        out = jnp.einsum(
            "bhqjk,bjhkd->bhqd", w_near, near[:, :, 1], preferred_element_type=jnp.float32
        )
        out = out + jnp.einsum(
            "bhqk,khd->bhqd", weights[..., 9 * BT :], far_vals, preferred_element_type=jnp.float32
        )
        return out.astype(jnp.bfloat16)

    heard = lax.map(attend, (q_groups, idx_groups)).reshape(blocks, HEADS, BT, HD)
    heard = heard.transpose(0, 2, 1, 3).reshape(-1, width)
    return jnp.dot(heard, w_out, preferred_element_type=jnp.float32).astype(jnp.bfloat16)


def solution(mesh):
    placed = (
        P(("face", "sub"), None),
        P(),
        P(),
        P(("face", "sub"), None),
        P(("face", "sub")),
        P(),
        P(),
    )
    return jax.shard_map(
        body, mesh=mesh, in_specs=placed, out_specs=P(("face", "sub"), None), check_vma=False
    )
```

profile of v0, /device:TPU:1, one launch (start us, length us, event | category | flops | bytes accessed | tf_op | source)
XLA Modules:
  0.0 738.6 jit_solution(11624246967768360266)
XLA Ops:
  8.1 9.6 %convolution_convert_fusion = bf16[1024,3072]{1,0:T(8,128)(2,1)S(1)} fusion(bf16[1024,1024]{1,0:T(8,128)(2,1)S(1)} %copy-done, bf16[1024,3072]{1,0:T(8,128)(2,1)} %param.10), kind=kOutput, calls=%fused_computation.28 | convolution fusion | flops 6445596672 | bytes 14680064 | tf_op jit(solution)/shard_map/dot_general | solution.py:43
  22.8 12.9 %reshape_reshape.3 = bf16[16,64,2,16,64]{4,3,2,1,0:T(8,128)(2,1)} reshape(bf16[1024,2048]{1,0:T(8,128)(2,1)} %slice.67) | data formatting | bytes 8388608 | tf_op jit(solution)/shard_map/reshape;reshape | solution.py:35
  35.7 7.2 slice_bitcast_fusion
  59.4 200.8 %all-reduce.2.cloned.1.call-done = f32[128,2048]{1,0:T(8,128)} async-done(((f32[128,2048]{1,0:T(8,128)}), f32[128,2048]{1,0:T(8,128)}) %all-reduce.2.cloned.1.call-update) | async-done | bytes 1048592 | tf_op jit(solution)/shard_map/psum | solution.py:68
  265.5 5.8 copy_dynamic-update-slice_fusion.2
  271.3 10.2 %copy_dynamic-update-slice_fusion = bf16[4,8,2,16,64,64]{5,4,3,2,1,0:T(8,128)(2,1)} fusion(bf16[4,8,2,16,64,64]{5,4,3,2,1,0:T(8,128)(2,1)} %copy_dynamic-update-slice_fusion.2, bf16[2,8,2,16,64,64]{5,3,2,4,1,0:T(8,128)(2,1)} %bitcast.130), kind=kLoop, calls=%fused_computation.27 | loop fusion | bytes 16777216
  281.4 5.8 copy_dynamic-update-slice_fusion.1
  296.7 45.9 %collective-permute-done.3 = bf16[4,1,2,16,64,64]{5,4,3,2,1,0:T(8,128)(2,1)} collective-permute-done((bf16[4,1,2,16,64,64]{5,4,3,2,1,0:T(8,128)(2,1)}, bf16[4,1,2,16,64,64]{5,4,3,2,1,0:T(8,128)(2,1)}, u32[]{:S(2)}, u32[]{:S(2)}) %collective-permute-start.3) | collective-permute-done | bytes 1048608 | tf_op jit(solution)/shard_map/ppermute | solution.py:21
  342.6 17.3 %pad_maximum_fusion = bf16[4,10,2,16,64,64]{5,4,3,2,1,0:T(8,128)(2,1)} fusion(bf16[4,1,2,16,64,64]{5,4,3,2,1,0:T(8,128)(2,1)} %collective-permute-done.3, bf16[4,8,2,16,64,64]{5,4,3,2,1,0:T(8,128)(2,1)} %copy_dynamic-update-slice_fusion.1, bf16[4,1,2,16,64,64]{5,4,3,2,1,0:T(8,128)(2,1)} %collective-permute-done.2), kind=kLoop, calls=%fused_computation.26 | loop fusion | flops 10485760 | bytes 20971520 | tf_op jit(solution)/shard_map/concatenate | solution.py:22
  359.9 351.4 %while.10 = (s32[]{:T(128)}, bf16[2,8,16,64,64]{4,3,2,1,0:T(8,128)(2,1)}, bf16[2,8,16,64,64]{4,3,2,1,0:T(8,128)(2,1)}, s32[2,8,9]{2,1,0:T(8,128)S(1)}, bf16[40,2...) while((s32[]{:T(128)}, ...), condition=%wide.region_7.8_spmd, body=%wide.region_3.7_spmd.sunk | while | flops 1600111872 | bytes 372686784 | solution.py:117
  360.1 20.4 %gather_fusion = bf16[72,2,16,64,64]{4,3,2,1,0:T(8,128)(2,1)} fusion(bf16[40,2,16,64,64]{4,3,2,1,0:T(8,128)(2,1)} %get-tuple-element.211, s32[1024]{0:T(1024)S(1)} %pad_clamp_fusion.2), kind=kCustom, calls=%fused_computation.clone.1 | custom fusion | bytes 37749024 | tf_op jit(solution)/shard_map/while/body/eval_jaxpr/gather | solution.py:95
  380.6 25.7 %fusion.64 = (bf16[8,9,1,16,64,64]{5,4,3,2,1,0:T(8,128)(2,1)}, bf16[8,9,1,16,64,64]{5,4,3,2,1,0:T(8,128)(2,1)}) fusion(bf16[8,9,2,16,64,64]{5,4,3,2,1,0:T(8,128)(2,1)} %bitcast.125), kind=kLoop, calls=%fused_computation.95.clone.1 | loop fusion | bytes 37748736 | tf_op jit(solution)/shard_map/while/body/eval_jaxpr/slice | solution.py:110
  406.3 19.5 %fusion.65 = (f32[8,16,64]{2,1,0:T(8,128)S(1)}, f32[8,16,64,9,64]{2,4,3,1,0:T(8,128)}) fusion(bf16[8,9,1,16,64,64]{5,4,3,2,1,0:T(8,128)(2,1)} %get-tuple-element.183, bf16[2,8,16,64,64]{4,3,2,1,0:T(8,128)(2,1)} %get-tuple-element.209, s32[]{:T(128)S(6)} %copy.159), kind=kOutput, calls=%fused_computation.96.clone.1 | convolution fusion | flops 613408768 | bytes 39878660 | tf_op jit(solution)/shard_map/while/body/eval_jaxpr/bhqd,bjhkd->bhqjk/dot_general | solution.py:97
  425.8 28.2 %copy.151 = f32[8,16,64,576]{3,2,1,0:T(8,128)} copy(f32[8,16,64,576]{2,3,1,0:T(8,128)} %bitcast.124) | data formatting | bytes 37748736 | tf_op jit(solution)/shard_map/while/body/eval_jaxpr/reshape | solution.py:100
  457.1 15.4 %fusion.67 = f32[8,16,64]{2,1,0:T(8,128)S(1)} fusion(f32[8,16,64,576]{3,2,1,0:T(8,128)} %copy.151, f32[8,16,64]{2,1,0:T(8,128)S(1)} %copy_maximum_fusion.2, f32[8,16,64,160]{3,2,0,1:T(8,128)S(1)} %get-tuple-element.187), kind=kLoop, calls=%fused_computation.9.clone.1 | loop fusion | flops 18079744 | bytes 24182784 | tf_op jit(solution)/shard_map/while/body/eval_jaxpr/reduce_sum | solution.py:105
  472.6 12.5 %divide_convert_fusion.2 = bf16[8,16,64,736]{3,2,1,0:T(8,128)(2,1)} fusion(f32[8,16,64,576]{3,2,1,0:T(8,128)S(1)} %bitcast.123, f32[8,16,64]{2,1,0:T(8,128)S(1)} %fusion.67, f32[8,16,64]{2,1,0:T(8,128)S(1)} %copy_maximum_fusion.2, f32[8,16,64,160]{3,2,0,1:T(8,128)S(1)} %get-tuple-element.187), kind=kLoop, calls=%fused_computation.3.clone.1 | loop fusion | flops 24117248 | bytes 36241408 | tf_op jit(solution)/shard_map/while/body/eval_jaxpr/convert_element_type | solution.py:105
  490.7 9.0 %slice.101 = bf16[8,16,64,576]{3,2,1,0:T(8,128)(2,1)} slice(bf16[8,16,64,736]{3,2,1,0:T(8,128)(2,1)} %divide_convert_fusion.2), slice={[0:8], [0:16], [0:64], [0:576]} | slice | bytes 18874368 | tf_op jit(solution)/shard_map/while/body/eval_jaxpr/slice | solution.py:108
  499.7 18.9 %copy.152 = bf16[8,16,64,576]{2,3,1,0:T(8,128)(2,1)} copy(bf16[8,16,64,576]{3,2,1,0:T(8,128)(2,1)} %slice.101) | data formatting | bytes 18874368 | tf_op jit(solution)/shard_map/while/body/eval_jaxpr/slice | solution.py:108
  518.7 16.9 %bitcast_dynamic-update-slice_fusion.2 = bf16[2,8,16,64,64]{4,3,2,1,0:T(8,128)(2,1)} fusion(bf16[2,8,16,64,64]{4,3,2,1,0:T(8,128)(2,1)} %get-tuple-element.199, s32[]{:T(128)S(6)} %copy.159, f32[16,8,64,64]{3,2,0,1:T(8,128)} %fusion.68, bf16[8,16,64,9,64]{2,4,3,1,0:T(8,128)(2,1)} %bitcast.127, bf16[8,9,1,16,64,64]{5,4,3,2,1,0:T(8,128)(2,1)} %get-tuple-element.188), kind=kOutput, calls=%fused_computation.16.clone.1 | convolution fusion | flops 605028352 | bytes 44040196 | tf_op jit(solution)/shard_map/while/body/eval_jaxpr/bhqjk,bjhkd->bhqd/dot_general | solution.py:109
  535.7 20.4 %gather_fusion = bf16[72,2,16,64,64]{4,3,2,1,0:T(8,128)(2,1)} fusion(bf16[40,2,16,64,64]{4,3,2,1,0:T(8,128)(2,1)} %get-tuple-element.211, s32[1024]{0:T(1024)S(1)} %pad_clamp_fusion.2), kind=kCustom, calls=%fused_computation.clone.1 | custom fusion | bytes 37749024 | tf_op jit(solution)/shard_map/while/body/eval_jaxpr/gather | solution.py:95
  556.1 25.7 %fusion.64 = (bf16[8,9,1,16,64,64]{5,4,3,2,1,0:T(8,128)(2,1)}, bf16[8,9,1,16,64,64]{5,4,3,2,1,0:T(8,128)(2,1)}) fusion(bf16[8,9,2,16,64,64]{5,4,3,2,1,0:T(8,128)(2,1)} %bitcast.125), kind=kLoop, calls=%fused_computation.95.clone.1 | loop fusion | bytes 37748736 | tf_op jit(solution)/shard_map/while/body/eval_jaxpr/slice | solution.py:110
  581.8 19.5 %fusion.65 = (f32[8,16,64]{2,1,0:T(8,128)S(1)}, f32[8,16,64,9,64]{2,4,3,1,0:T(8,128)}) fusion(bf16[8,9,1,16,64,64]{5,4,3,2,1,0:T(8,128)(2,1)} %get-tuple-element.183, bf16[2,8,16,64,64]{4,3,2,1,0:T(8,128)(2,1)} %get-tuple-element.209, s32[]{:T(128)S(6)} %copy.159), kind=kOutput, calls=%fused_computation.96.clone.1 | convolution fusion | flops 613408768 | bytes 39878660 | tf_op jit(solution)/shard_map/while/body/eval_jaxpr/bhqd,bjhkd->bhqjk/dot_general | solution.py:97
  601.4 28.2 %copy.151 = f32[8,16,64,576]{3,2,1,0:T(8,128)} copy(f32[8,16,64,576]{2,3,1,0:T(8,128)} %bitcast.124) | data formatting | bytes 37748736 | tf_op jit(solution)/shard_map/while/body/eval_jaxpr/reshape | solution.py:100
  632.7 15.4 %fusion.67 = f32[8,16,64]{2,1,0:T(8,128)S(1)} fusion(f32[8,16,64,576]{3,2,1,0:T(8,128)} %copy.151, f32[8,16,64]{2,1,0:T(8,128)S(1)} %copy_maximum_fusion.2, f32[8,16,64,160]{3,2,0,1:T(8,128)S(1)} %get-tuple-element.187), kind=kLoop, calls=%fused_computation.9.clone.1 | loop fusion | flops 18079744 | bytes 24182784 | tf_op jit(solution)/shard_map/while/body/eval_jaxpr/reduce_sum | solution.py:105
  648.1 12.5 %divide_convert_fusion.2 = bf16[8,16,64,736]{3,2,1,0:T(8,128)(2,1)} fusion(f32[8,16,64,576]{3,2,1,0:T(8,128)S(1)} %bitcast.123, f32[8,16,64]{2,1,0:T(8,128)S(1)} %fusion.67, f32[8,16,64]{2,1,0:T(8,128)S(1)} %copy_maximum_fusion.2, f32[8,16,64,160]{3,2,0,1:T(8,128)S(1)} %get-tuple-element.187), kind=kLoop, calls=%fused_computation.3.clone.1 | loop fusion | flops 24117248 | bytes 36241408 | tf_op jit(solution)/shard_map/while/body/eval_jaxpr/convert_element_type | solution.py:105
  660.7 5.6 fusion.68
  666.3 9.0 %slice.101 = bf16[8,16,64,576]{3,2,1,0:T(8,128)(2,1)} slice(bf16[8,16,64,736]{3,2,1,0:T(8,128)(2,1)} %divide_convert_fusion.2), slice={[0:8], [0:16], [0:64], [0:576]} | slice | bytes 18874368 | tf_op jit(solution)/shard_map/while/body/eval_jaxpr/slice | solution.py:108
  675.3 18.9 %copy.152 = bf16[8,16,64,576]{2,3,1,0:T(8,128)(2,1)} copy(bf16[8,16,64,576]{3,2,1,0:T(8,128)(2,1)} %slice.101) | data formatting | bytes 18874368 | tf_op jit(solution)/shard_map/while/body/eval_jaxpr/slice | solution.py:108
  694.2 16.9 %bitcast_dynamic-update-slice_fusion.2 = bf16[2,8,16,64,64]{4,3,2,1,0:T(8,128)(2,1)} fusion(bf16[2,8,16,64,64]{4,3,2,1,0:T(8,128)(2,1)} %get-tuple-element.199, s32[]{:T(128)S(6)} %copy.159, f32[16,8,64,64]{3,2,0,1:T(8,128)} %fusion.68, bf16[8,16,64,9,64]{2,4,3,1,0:T(8,128)(2,1)} %bitcast.127, bf16[8,9,1,16,64,64]{5,4,3,2,1,0:T(8,128)(2,1)} %get-tuple-element.188), kind=kOutput, calls=%fused_computation.16.clone.1 | convolution fusion | flops 605028352 | bytes 44040196 | tf_op jit(solution)/shard_map/while/body/eval_jaxpr/bhqjk,bjhkd->bhqd/dot_general | solution.py:109
  711.3 7.7 %copy.136 = bf16[16,16,64,64]{3,1,2,0:T(8,128)(2,1)} copy(bf16[16,16,64,64]{3,2,1,0:T(8,128)(2,1)} %bitcast.135) | data formatting | bytes 4194304 | tf_op jit(solution)/shard_map/reshape | solution.py:117
  719.0 6.7 reshape.104
  725.6 5.9 convolution_convert_fusion.1
  (92 shorter events, 49.6 us)
Async XLA Ops:
  6.5 1.6 copy-start
  6.5 253.7 %all-reduce.2.cloned.1.call-start = ((), (), s32[]{:S(2)}) async-start(), calls=%async_computation | async-start | bytes 2097152 | tf_op jit(solution)/shard_map/psum | solution.py:68
  17.8 2.7 copy-start.3
  35.7 11.9 %copy-start.4 = (bf16[1024,3072]{1,0:T(8,128)(2,1)S(1)}, bf16[1024,3072]{1,0:T(8,128)(2,1)}, u32[]{:S(2)}) copy-start(bf16[1024,3072]{1,0:T(8,128)(2,1)} %copy-done.3) | copy-start | bytes 18874372
  35.7 11.9 %copy-start.8 = (s32[1024]{0:T(1024)S(1)}, s32[1024]{0:T(1024)}, u32[]{:S(2)}) copy-start(s32[1024]{0:T(1024)} %param.13) | copy-start | bytes 12292
  42.9 6.6 slice-start.5
  42.9 222.6 %collective-permute-start = (bf16[1,8,2,16,64,64]{5,3,2,4,1,0:T(8,128)(2,1)}, bf16[1,8,2,16,64,64]{5,3,2,4,1,0:T(8,128)(2,1)}, u32[]{:S(2)}, u32[]{:S(2)}) collective-permute-start(bf16[1,8,2,16,64,64]{5,3,2,4,1,0:T(8,128)(2,1)} %get-tuple-element.121), channel_id=1, source_target_pairs={{0,16},{16,32},{32,48},{48,64},{64,80},{80,96},{96,112},{112,0},{1... | collective-permute-start | bytes 6291464 | tf_op jit(solution)/shard_map/ppermute | solution.py:18
  44.9 236.5 %collective-permute-start.1 = (bf16[1,8,2,16,64,64]{5,3,2,4,1,0:T(8,128)(2,1)}, bf16[1,8,2,16,64,64]{5,3,2,4,1,0:T(8,128)(2,1)}, u32[]{:S(2)}, u32[]{:S(2)}) collective-permute-start(bf16[1,8,2,16,64,64]{5,3,2,4,1,0:T(8,128)(2,1)} %get-tuple-element.120), channel_id=1, source_target_pairs={{16,0},{32,16},{48,32},{64,48},{80,64},{96,80},{112,96},{0,112},{1... | collective-permute-start | bytes 6291464 | tf_op jit(solution)/shard_map/ppermute | solution.py:21
  49.4 9.7 %copy-start.6 = (f32[2,16]{1,0:T(2,128)S(1)}, f32[2,16]{1,0:T(2,128)}, u32[]{:S(2)}) copy-start(f32[2,16]{1,0:T(2,128)} %param.15) | copy-start | bytes 388
  49.4 9.9 %copy-start.5 = (s32[16,9]{1,0:T(8,128)S(1)}, s32[16,9]{1,0:T(8,128)}, u32[]{:S(2)}) copy-start(s32[16,9]{1,0:T(8,128)} %param.12) | copy-start | bytes 1732
  49.4 210.8 %copy-start.7 = (s32[128]{0:T(128)S(1)}, s32[128]{0:T(128)}, u32[]{:S(2)}) copy-start(s32[128]{0:T(128)} %param.14) | copy-start | bytes 1540
  281.4 14.7 %copy-start.2 = (f32[128,2048]{1,0:T(8,128)S(1)}, f32[128,2048]{1,0:T(8,128)}, u32[]{:S(2)}) copy-start(f32[128,2048]{1,0:T(8,128)} %all-reduce.2.cloned.1.call-done) | copy-start | bytes 3145732
  292.8 49.8 %collective-permute-start.3 = (bf16[4,1,2,16,64,64]{5,4,3,2,1,0:T(8,128)(2,1)}, bf16[4,1,2,16,64,64]{5,4,3,2,1,0:T(8,128)(2,1)}, u32[]{:S(2)}, u32[]{:S(2)}) collective-permute-start(bf16[4,1,2,16,64,64]{5,4,3,2,1,0:T(8,128)(2,1)} %get-tuple-element.119), channel_id=1, source_target_pairs={{1,0},{2,1},{3,2},{4,3},{5,4},{6,5},{7,6},{8,7},{9,8},{10,9},{11,1... | collective-permute-start | bytes 3145736 | tf_op jit(solution)/shard_map/ppermute | solution.py:21
  292.8 49.8 %collective-permute-start.2 = (bf16[4,1,2,16,64,64]{5,4,3,2,1,0:T(8,128)(2,1)}, bf16[4,1,2,16,64,64]{5,4,3,2,1,0:T(8,128)(2,1)}, u32[]{:S(2)}, u32[]{:S(2)}) collective-permute-start(bf16[4,1,2,16,64,64]{5,4,3,2,1,0:T(8,128)(2,1)} %get-tuple-element.118), channel_id=1, source_target_pairs={{0,1},{1,2},{2,3},{3,4},{4,5},{5,6},{6,7},{7,8},{8,9},{9,10},{10,1... | collective-permute-start | bytes 3145736 | tf_op jit(solution)/shard_map/ppermute | solution.py:18
  454.0 18.5 %slice-start = ((s8[20971520]{0:T(1024)(128)(4,1)}), s8[4194304]{0:T(1024)(128)(4,1)S(1)}, s32[]{:S(2)}) async-start(s8[20971520]{0:T(1024)(128)(4,1)} %bitcast.122), calls=%async_computation.1 | async-start | bytes 8388608 | tf_op jit(solution)/shard_map/while
  454.0 18.5 %slice-start.1 = ((s8[20971520]{0:T(1024)(128)(4,1)}), s8[4194304]{0:T(1024)(128)(4,1)S(1)}, s32[]{:S(2)}) async-start(s8[20971520]{0:T(1024)(128)(4,1)} %bitcast.122), calls=%async_computation.2 | async-start | bytes 8388608 | tf_op jit(solution)/shard_map/while
  457.1 15.4 %slice-start.2 = ((s8[20971520]{0:T(1024)(128)(4,1)}), s8[4194304]{0:T(1024)(128)(4,1)S(1)}, s32[]{:S(2)}) async-start(s8[20971520]{0:T(1024)(128)(4,1)} %bitcast.122), calls=%async_computation.3 | async-start | bytes 8388608 | tf_op jit(solution)/shard_map/while
  457.1 15.4 %slice-start.3 = ((s8[20971520]{0:T(1024)(128)(4,1)}), s8[4194304]{0:T(1024)(128)(4,1)S(1)}, s32[]{:S(2)}) async-start(s8[20971520]{0:T(1024)(128)(4,1)} %bitcast.122), calls=%async_computation.4 | async-start | bytes 8388608 | tf_op jit(solution)/shard_map/while
  457.1 15.4 %slice-start.4 = ((s8[20971520]{0:T(1024)(128)(4,1)}), s8[4194304]{0:T(1024)(128)(4,1)S(1)}, s32[]{:S(2)}) async-start(s8[20971520]{0:T(1024)(128)(4,1)} %bitcast.122), calls=%async_computation.5 | async-start | bytes 8388608 | tf_op jit(solution)/shard_map/while
  629.6 18.5 %slice-start = ((s8[20971520]{0:T(1024)(128)(4,1)}), s8[4194304]{0:T(1024)(128)(4,1)S(1)}, s32[]{:S(2)}) async-start(s8[20971520]{0:T(1024)(128)(4,1)} %bitcast.122), calls=%async_computation.1 | async-start | bytes 8388608 | tf_op jit(solution)/shard_map/while
  629.6 18.5 %slice-start.1 = ((s8[20971520]{0:T(1024)(128)(4,1)}), s8[4194304]{0:T(1024)(128)(4,1)S(1)}, s32[]{:S(2)}) async-start(s8[20971520]{0:T(1024)(128)(4,1)} %bitcast.122), calls=%async_computation.2 | async-start | bytes 8388608 | tf_op jit(solution)/shard_map/while
  632.6 15.4 %slice-start.2 = ((s8[20971520]{0:T(1024)(128)(4,1)}), s8[4194304]{0:T(1024)(128)(4,1)S(1)}, s32[]{:S(2)}) async-start(s8[20971520]{0:T(1024)(128)(4,1)} %bitcast.122), calls=%async_computation.3 | async-start | bytes 8388608 | tf_op jit(solution)/shard_map/while
  632.6 15.4 %slice-start.3 = ((s8[20971520]{0:T(1024)(128)(4,1)}), s8[4194304]{0:T(1024)(128)(4,1)S(1)}, s32[]{:S(2)}) async-start(s8[20971520]{0:T(1024)(128)(4,1)} %bitcast.122), calls=%async_computation.4 | async-start | bytes 8388608 | tf_op jit(solution)/shard_map/while
  632.7 15.4 %slice-start.4 = ((s8[20971520]{0:T(1024)(128)(4,1)}), s8[4194304]{0:T(1024)(128)(4,1)S(1)}, s32[]{:S(2)}) async-start(s8[20971520]{0:T(1024)(128)(4,1)} %bitcast.122), calls=%async_computation.5 | async-start | bytes 8388608 | tf_op jit(solution)/shard_map/while
  719.0 12.6 %copy-start.1 = (bf16[1024,1024]{1,0:T(8,128)(2,1)S(1)}, bf16[1024,1024]{1,0:T(8,128)(2,1)}, u32[]{:S(2)}) copy-start(bf16[1024,1024]{1,0:T(8,128)(2,1)} %param.9) | copy-start | bytes 6291460
Sparse Core Ops, SparseCore 0:
  49.5 210.6 all-reduce.1
where the time goes:
time: 747 us; the launch traced here: 739 us
  local copies, waits for them, and re-layouts  285 us (38%)
  waiting for transfers between devices  247 us (33%)
  matrix products  109 us (15%)
  other arithmetic  75.5 us (10%)
  between operations  13.8 us (2%)
  starting transfers between devices  7.99 us (1%)
    psum x1, waiting for transfers between devices, body(): sums_one = lax.psum(partial_value, ('face', 'sub'))  201 us
    reshape x2, local copies, waits for them, and re-layouts, attend(): s_near = s_near.reshape(8, HEADS, BT, 9 * BT)  56.4 us
    slice x4, local copies, waits for them, and re-layouts, attend(): w_near = weights[..., :9 * BT].reshape(8, HEADS, BT, 9, BT)  55.9 us
    slice x2, local copies, waits for them, and re-layouts, attend(): near[:, :, 1]  51.4 us
    ppermute x2, waiting for transfers between devices, padded(): lax.ppermute(lax.slice_in_dim(block, 0, width, axis=dim), axis, backward)  45.9 us
    gather x2, local copies, waits for them, and re-layouts, attend(): near = ext_flat[ib]  40.9 us
    dot_general x2, matrix products, attend(): jnp.einsum('bhqd,bjhkd->bhqjk', qb, near[:, :, 0], preferred_element_type...  39.1 us
    dot_general x2, matrix products, attend(): jnp.einsum('bhqjk,bjhkd->bhqd', w_near, near[:, :, 1], preferred_element_...  33.8 us
  transfers between devices with their start and end apart: 5, of which 2 were waited for; matrix products, arithmetic and copies ran while one was open for 5% of the time, Pallas kernels for 0%

commit v1 on v0

v1 whole, which is shorter than its diff:
```python
import functools

import jax
import jax.numpy as jnp
from jax import lax
from jax.experimental import pallas as pl
from jax.experimental.pallas import tpu as pltpu
from jax.sharding import PartitionSpec as P

D = 1024
HEADS = 16
HD = 64
BT = 64
BR = 2
BC = 8
GROUP = 4
GW = GROUP * HD
WIDE = BC + 2
EXT_ROW = WIDE * BT
EXT = (BR + 2) * EXT_ROW
ROW = BC * BT
LOG2E = 1.4426950408889634
MESH = pl.DeviceIdType.MESH
BF = jnp.bfloat16
F32 = jnp.float32


def kernel(
    n_face,
    n_sub,
    x_ref,
    wqkv_ref,
    wout_ref,
    near_ref,
    bias_ref,
    out_ref,
    xe,
    wq,
    wo,
    q,
    kv,
    heard,
    mixed,
    part,
    cells,
    far,
    load_sem,
    store_sem,
    halo_send,
    halo_recv,
    part_send,
    part_recv,
    cell_send,
    cell_recv,
):
    face = lax.axis_index("face")
    sub = lax.axis_index("sub")
    up = lax.rem(face + n_face - 1, n_face)
    down = lax.rem(face + 1, n_face)
    left = lax.rem(sub + n_sub - 1, n_sub)
    right = lax.rem(sub + 1, n_sub)
    n_one = n_sub * 8
    n_two = n_sub * 2
    n_far = n_one + n_two

    peers = [(lax.rem(face + d, n_face), sub) for d in range(1, n_face)]
    peers += [(face, lax.rem(sub + d, n_sub)) for d in range(1, n_sub)]
    peers += [(up, left), (up, right), (down, left), (down, right)]
    barrier = pltpu.get_barrier_semaphore()
    for peer in peers:
        pl.semaphore_signal(barrier, inc=1, device_id=peer, device_id_type=MESH)

    own = [(EXT_ROW + BT, 0), (2 * EXT_ROW + BT, ROW)]
    loads = []
    for i, (to, at) in enumerate(own):
        loads.append(
            pltpu.make_async_copy(
                x_ref.at[pl.ds(at, ROW)], xe.at[pl.ds(to, ROW)], load_sem.at[i]
            )
        )
    loads.append(pltpu.make_async_copy(wqkv_ref, wq, load_sem.at[2]))
    loads.append(pltpu.make_async_copy(wout_ref, wo, load_sem.at[3]))
    for load in loads:
        load.start()

    pl.semaphore_wait(barrier, len(peers))

    last = ROW - BT
    sends = [
        (0, BT, 3 * EXT_ROW + 9 * BT, (up, left)),
        (last, BT, 3 * EXT_ROW, (up, right)),
        (ROW, BT, 9 * BT, (down, left)),
        (ROW + last, BT, 0, (down, right)),
        (0, ROW, 3 * EXT_ROW + BT, (up, sub)),
        (ROW, ROW, BT, (down, sub)),
        (0, BT, EXT_ROW + 9 * BT, (face, left)),
        (ROW, BT, 2 * EXT_ROW + 9 * BT, (face, left)),
        (last, BT, EXT_ROW, (face, right)),
        (ROW + last, BT, 2 * EXT_ROW, (face, right)),
    ]
    halos = []
    for i, (at, rows, to, peer) in enumerate(sends):
        halos.append(
            pltpu.make_async_remote_copy(
                src_ref=x_ref.at[pl.ds(at, rows)],
                dst_ref=xe.at[pl.ds(to, rows)],
                send_sem=halo_send.at[i],
                recv_sem=halo_recv.at[i],
                device_id=peer,
                device_id_type=MESH,
            )
        )
    for halo in halos:
        halo.start()

    loads[0].wait()
    loads[1].wait()
    for half in range(2):
        total = None
        for to, _ in own:
            tok = xe[pl.ds(to + half * (ROW // 2), ROW // 2), :].astype(F32)
            s = jnp.sum(tok, axis=0, keepdims=True)
            total = s if total is None else total + s
        part[face, pl.ds(half, 1), :] = total
    parts = []
    for d in range(1, n_face):
        parts.append(
            pltpu.make_async_remote_copy(
                src_ref=part.at[face],
                dst_ref=part.at[face],
                send_sem=part_send.at[d],
                recv_sem=part_recv.at[d],
                device_id=(lax.rem(face + d, n_face), sub),
                device_id_type=MESH,
            )
        )
    for copy in parts:
        copy.start()

    loads[2].wait()

    def own_query(n, carry):
        cols = pl.ds(pl.multiple_of(n * GW, GW), GW)
        for to, at in own:
            y = jnp.dot(xe[pl.ds(to, ROW), :], wq[:, cols], preferred_element_type=F32)
            q[pl.ds(at, ROW), cols] = (y * (HD**-0.5 * LOG2E)).astype(BF)
        return carry

    lax.fori_loop(0, D // GW, own_query, 0)

    for copy in parts:
        copy.wait()
    for k in range(n_face // 2):
        cells[sub, pl.ds(2 * k, 2), :] = part[2 * k] + part[2 * k + 1]
    gathers = []
    for d in range(1, n_sub):
        gathers.append(
            pltpu.make_async_remote_copy(
                src_ref=cells.at[sub],
                dst_ref=cells.at[sub],
                send_sem=cell_send.at[d],
                recv_sem=cell_recv.at[d],
                device_id=(face, lax.rem(sub + d, n_sub)),
                device_id_type=MESH,
            )
        )
    for copy in gathers:
        copy.start()

    def pairs_of(start, rows):
        def step(n, carry):
            cols = pl.ds(pl.multiple_of(n * GW, GW), GW)
            wcols = pl.ds(pl.multiple_of(D + n * GW, GW), GW)
            y = jnp.dot(xe[pl.ds(start, rows), :], wq[:, wcols], preferred_element_type=F32)
            kv[pl.ds(start, rows), cols] = y.astype(BF)
            return carry

        lax.fori_loop(0, 2 * D // GW, step, 0)

    for to, _ in own:
        pairs_of(to, ROW)

    for copy in gathers:
        copy.wait()

    one = cells[...].reshape(n_one, D)
    one_hi = one.astype(BF)
    one_lo = (one - one_hi.astype(F32)).astype(BF)
    pick = (
        lax.broadcasted_iota(jnp.int32, (n_two, n_one), 1) // 4
        == lax.broadcasted_iota(jnp.int32, (n_two, n_one), 0)
    ).astype(BF)
    two = jnp.dot(pick, one_hi, preferred_element_type=F32) + jnp.dot(
        pick, one_lo, preferred_element_type=F32
    )
    two_hi = two.astype(BF)
    two_lo = (two - two_hi.astype(F32)).astype(BF)
    sums = jnp.concatenate([one_hi, two_hi, one_lo, two_lo], axis=0)
    same = (
        lax.broadcasted_iota(jnp.int32, (GW, GW), 0) // HD
        == lax.broadcasted_iota(jnp.int32, (GW, GW), 1) // HD
    )
    mean = jnp.where(same, 1.0 / HD, 0.0).astype(BF)

    def pooled(n, carry):
        cols = pl.ds(pl.multiple_of(n * GW, GW), GW)
        wcols = pl.ds(pl.multiple_of(D + n * GW, GW), GW)
        y = jnp.dot(sums, wq[:, wcols], preferred_element_type=F32)
        y = y[:n_far] + y[n_far:]
        sq = jnp.dot((y * y).astype(BF), mean, preferred_element_type=F32)
        far[:, cols] = (y * lax.rsqrt(sq + 1e-5)).astype(BF)
        return carry

    lax.fori_loop(0, 2 * D // GW, pooled, 0)

    for halo in halos:
        halo.wait()
    pairs_of(0, EXT_ROW + BT)
    pairs_of(2 * EXT_ROW - BT, 2 * BT)
    pairs_of(3 * EXT_ROW - BT, EXT_ROW + BT)

    lane = lax.broadcasted_iota(jnp.int32, (BT, GW), 1) // HD
    lane_far = lax.broadcasted_iota(jnp.int32, (BT, 128), 1)

    def attend(b, carry):
        corner = b // BC * EXT_ROW + b % BC * BT
        me = corner + EXT_ROW + BT
        own_id = near_ref[b, 4]
        starts = []
        for j in range(9):
            at = corner + j // 3 * EXT_ROW + j % 3 * BT
            if j in (0, 2, 6, 8):
                other = near_ref[b, j] - own_id
                at = me + (at - me) * jnp.minimum(other * other, 1)
            starts.append(at)
        rows = pl.ds(pl.multiple_of(b * BT, BT), BT)
        for g in range(HEADS // GROUP):
            cols = pl.ds(g * GW, GW)
            vcols = pl.ds(D + g * GW, GW)
            qb = q[rows, cols]
            zero = jnp.zeros_like(qb)
            qs = jnp.concatenate([jnp.where(lane == h, qb, zero) for h in range(GROUP)], axis=0)
            keys = jnp.concatenate(
                [far[:, cols]] + [kv[pl.ds(at, BT), cols] for at in starts], axis=0
            )
            vals = jnp.concatenate(
                [far[:, vcols]] + [kv[pl.ds(at, BT), vcols] for at in starts], axis=0
            )
            s = lax.dot_general(
                qs, keys, (((1,), (1,)), ((), ())), preferred_element_type=F32
            )
            add_one = jnp.concatenate(
                [jnp.full((BT, 128), bias_ref[0, g * GROUP + h] * LOG2E, F32) for h in range(GROUP)],
                axis=0,
            )
            add_two = jnp.concatenate(
                [
                    jnp.where(lane_far < n_two, bias_ref[1, g * GROUP + h] * LOG2E, 0.0)
                    for h in range(GROUP)
                ],
                axis=0,
            )
            s = jnp.concatenate(
                [s[:, :128] + add_one, s[:, 128:256] + add_two, s[:, 256:]], axis=1
            )
            p = jnp.exp2(s - jnp.max(s, axis=1, keepdims=True))
            total = jnp.sum(p, axis=1, keepdims=True)
            o = jnp.dot(p.astype(BF), vals, preferred_element_type=F32)
            o = o * (1.0 / total)
            h01 = jnp.where(lane == 0, o[:BT], o[BT : 2 * BT])
            h23 = jnp.where(lane == 2, o[2 * BT : 3 * BT], o[3 * BT :])
            heard[rows, cols] = jnp.where(lane < 2, h01, h23).astype(BF)
        return carry

    lax.fori_loop(0, BR * BC, attend, 0)

    loads[3].wait()

    def project(n, carry):
        cols = pl.ds(pl.multiple_of(n * GW, GW), GW)
        y = jnp.dot(heard[...], wo[:, cols], preferred_element_type=F32)
        mixed[:, cols] = y.astype(BF)
        return carry

    lax.fori_loop(0, D // GW, project, 0)
    store = pltpu.make_async_copy(mixed, out_ref, store_sem)
    store.start()
    store.wait()


def solution(mesh):
    n_face, n_sub = mesh.shape["face"], mesh.shape["sub"]
    tokens = BR * ROW
    n_far = n_sub * 10

    def body(x, w_qkv, w_out, neighbours, parent_one, parent_two, level_bias):
        call = pl.pallas_call(
            functools.partial(kernel, n_face, n_sub),
            out_shape=jax.ShapeDtypeStruct((tokens, D), BF),
            in_specs=[pl.BlockSpec(memory_space=pl.ANY)] * 3
            + [pl.BlockSpec(memory_space=pltpu.SMEM)] * 2,
            out_specs=pl.BlockSpec(memory_space=pl.ANY),
            scratch_shapes=[
                pltpu.VMEM((EXT, D), BF),
                pltpu.VMEM((D, 3 * D), BF),
                pltpu.VMEM((D, D), BF),
                pltpu.VMEM((tokens, D), BF),
                pltpu.VMEM((EXT, 2 * D), BF),
                pltpu.VMEM((tokens, D), BF),
                pltpu.VMEM((tokens, D), BF),
                pltpu.VMEM((n_face, 2, D), F32),
                pltpu.VMEM((n_sub, 8, D), F32),
                pltpu.VMEM((n_far, 2 * D), BF),
                pltpu.SemaphoreType.DMA((4,)),
                pltpu.SemaphoreType.DMA,
                pltpu.SemaphoreType.DMA((10,)),
                pltpu.SemaphoreType.DMA((10,)),
                pltpu.SemaphoreType.DMA((n_face,)),
                pltpu.SemaphoreType.DMA((n_face,)),
                pltpu.SemaphoreType.DMA((n_sub,)),
                pltpu.SemaphoreType.DMA((n_sub,)),
            ],
            compiler_params=pltpu.CompilerParams(
                collective_id=0, has_side_effects=True, vmem_limit_bytes=56 * 1024 * 1024
            ),
            cost_estimate=pl.CostEstimate(
                flops=60_000_000_000, bytes_accessed=16_000_000, transcendentals=12_000_000
            ),
        )
        return call(x, w_qkv, w_out, neighbours, level_bias)

    placed = (
        P(("face", "sub"), None),
        P(),
        P(),
        P(("face", "sub"), None),
        P(("face", "sub")),
        P(),
        P(),
    )
    return jax.shard_map(
        body, mesh=mesh, in_specs=placed, out_specs=P(("face", "sub"), None), check_vma=False
    )
```

time: 747 us -> 102 us (0.14); the launches traced: 739 us -> 101 us
  local copies, waits for them, and re-layouts: 285 us -> 3.08 us
  waiting for transfers between devices: 247 us -> 0 us
  matrix products: 109 us -> 0 us
  Pallas kernels: 0 us -> 98.4 us
  other arithmetic: 75.5 us -> 0 us
  between operations: 13.8 us -> 0.01 us
  starting transfers between devices: 7.99 us -> 0 us
    psum x1 -> x0, waiting for transfers between devices: 201 us -> none  [body(): sums_one = lax.psum(partial_value, ('face', 'sub'))]
    slice x11 -> x0, local copies, waits for them, and re-layouts: 122 us -> none  [the longest x4 55.9 us: attend(): w_near = weights[..., :9 * BT].reshape(8, HEADS, BT, 9, BT)]
    dot_general x12 -> x0, matrix products: 109 us -> none  [the longest x2 39.1 us: attend(): jnp.einsum('bhqd,bjhkd->bhqjk', qb, near[:, :, 0], preferred_element_type...]
    pallas_call x0 -> x1, Pallas kernels: none -> 98.4 us  [body(): return call(x, w_qkv, w_out, neighbours, level_bias)]
    reshape x5 -> x0, local copies, waits for them, and re-layouts: 75.1 us -> none  [the longest x2 56.4 us: attend(): s_near = s_near.reshape(8, HEADS, BT, 9 * BT)]
    ppermute x4 -> x0, waiting for transfers between devices: 45.9 us -> none  [the longest x2 45.9 us: padded(): lax.ppermute(lax.slice_in_dim(block, 0, width, axis=dim), axis, backward)]
    gather x2 -> x0, local copies, waits for them, and re-layouts: 40.9 us -> none  [attend(): near = ext_flat[ib]]
    reduce_sum x4 -> x0, other arithmetic: 31.1 us -> none  [the longest x2 30.8 us: attend(): jax.nn.softmax(jnp.concatenate([s_near, s_far], axis=-1), axis=-1)]
  transfers between devices with their start and end apart: 5 -> 0, of which waited for: 2 -> 0; matrix products, arithmetic and copies ran while one was open for 5% -> 0% of each run, Pallas kernels for 0% -> 0%
where the time goes in v1:
time: 102 us; the launch traced here: 101 us
  Pallas kernels  98.4 us (96%)
  local copies, waits for them, and re-layouts  3.08 us (3%)
    pallas_call x1, Pallas kernels, body(): return call(x, w_qkv, w_out, neighbours, level_bias)  98.4 us
    unnamed x1, local copies, waits for them, and re-layouts  3.08 us

profile of v1, /device:TPU:1, one launch (start us, length us, event | category | flops | bytes accessed | tf_op | source)
XLA Modules:
  0.0 101.5 jit_solution(1287923667336151106)
XLA Ops:
  0.0 98.4 %shard_map.55 = bf16[1024,1024]{1,0:T(8,128)(2,1)} custom-call(bf16[1024,1024]{1,0:T(8,128)(2,1)} %x_ref.1, bf16[1024,3072]{1,0:T(8,128)(2,1)} %wqkv_ref.1, bf16[1024,1024]{1,0:T(8,128)(2,1)} %wout_ref.1, s32[16,9]{1,0:T(8,128)} %near_ref.1, f32[2,16]{1,0:T(2,128)} %bias_ref.1), custom_call_target="tpu_custom_call" | custom-call | flops 60000002048 | bytes 16000000 | tf_op jit(solution)/shard_map/pallas_call | solution.py:330
  98.4 3.1 %copy.7 = bf16[1024,1024]{1,0:T(8,128)(2,1)} copy(bf16[1024,1024]{1,0:T(8,128)(2,1)} %shard_map.55) | data formatting | bytes 4194304

commit v2 on v1

v2 whole, which is shorter than its diff:
```python
import functools

import jax
import jax.numpy as jnp
from jax import lax
from jax.experimental import pallas as pl
from jax.experimental.pallas import tpu as pltpu
from jax.sharding import PartitionSpec as P

D = 1024
HEADS = 16
HD = 64
BT = 64
BR = 2
BC = 8
GROUP = 4
GW = GROUP * HD
WIDE = BC + 2
EXT_ROW = WIDE * BT
EXT = (BR + 2) * EXT_ROW
ROW = BC * BT
LOG2E = 1.4426950408889634
MESH = pl.DeviceIdType.MESH
BF = jnp.bfloat16
F32 = jnp.float32


def kernel(
    n_face,
    n_sub,
    x_ref,
    wqkv_ref,
    wout_ref,
    near_ref,
    bias_ref,
    out_ref,
    xe,
    wq,
    wo,
    q,
    kv,
    heard,
    mixed,
    part,
    cells,
    far,
    load_sem,
    store_sem,
    halo_send,
    halo_recv,
    part_send,
    part_recv,
    cell_send,
    cell_recv,
):
    face = lax.axis_index("face")
    sub = lax.axis_index("sub")
    up = lax.rem(face + n_face - 1, n_face)
    down = lax.rem(face + 1, n_face)
    left = lax.rem(sub + n_sub - 1, n_sub)
    right = lax.rem(sub + 1, n_sub)
    n_one = n_sub * 8
    n_two = n_sub * 2
    n_far = n_one + n_two

    core = lax.rem(sub, 2)
    high = lax.rem(sub // 2, 2)
    mate = sub + 1 - 2 * core
    across = sub + 2 - 4 * high
    along = [lax.rem(sub + d, n_sub) for d in range(4, n_sub, 4)]
    n_y = n_sub // 4
    shelf = core * (2 * n_y) + sub // 4 * 2
    slot = shelf + high

    peers = [(lax.rem(face + d, n_face), sub) for d in range(1, n_face)]
    peers += [(face, left), (face, right), (face, across)] + [(face, far_y) for far_y in along]
    barrier = pltpu.get_barrier_semaphore()
    for peer in peers:
        pl.semaphore_signal(barrier, inc=1, device_id=peer, device_id_type=MESH)

    own = [(EXT_ROW + BT, 0), (2 * EXT_ROW + BT, ROW)]
    loads = []
    for i, (to, at) in enumerate(own):
        loads.append(
            pltpu.make_async_copy(
                x_ref.at[pl.ds(at, ROW)], xe.at[pl.ds(to, ROW)], load_sem.at[i]
            )
        )
    for i in range(3):
        cols = pl.ds(i * D, D)
        loads.append(
            pltpu.make_async_copy(wqkv_ref.at[:, cols], wq.at[:, cols], load_sem.at[2 + i])
        )
    loads.append(pltpu.make_async_copy(wout_ref, wo, load_sem.at[5]))
    for load in loads:
        load.start()

    loads[0].wait()
    loads[1].wait()
    for half in range(2):
        total = None
        for to, _ in own:
            tok = xe[pl.ds(to + half * (ROW // 2), ROW // 2), :].astype(F32)
            s = jnp.sum(tok, axis=0, keepdims=True)
            total = s if total is None else total + s
        part[face, pl.ds(half, 1), :] = total

    def matmul(row_starts, rows, first, out, out_starts, out_first, width, scale):
        def step(n, carry):
            wcols = pl.ds(pl.multiple_of(first + n * width, width), width)
            cols = pl.ds(pl.multiple_of(out_first + n * width, width), width)
            x = [xe[pl.ds(at, rows), :] for at in row_starts]
            x = x[0] if len(x) == 1 else jnp.concatenate(x, axis=0)
            y = jnp.dot(x, wq[:, wcols], preferred_element_type=F32)
            if scale is not None:
                y = y * scale
            y = y.astype(BF)
            for i, at in enumerate(out_starts):
                out[pl.ds(at, rows), cols] = y[i * rows : (i + 1) * rows]
            return carry

        return step

    own_at = [to for to, _ in own]
    loads[2].wait()
    lax.fori_loop(
        0, 2, matmul(own_at, ROW, 0, q, [0, ROW], 0, 512, HD**-0.5 * LOG2E), 0
    )
    loads[3].wait()
    lax.fori_loop(0, 2, matmul(own_at, ROW, D, kv, own_at, 0, 512, None), 0)
    loads[4].wait()

    pl.semaphore_wait(barrier, len(peers))

    parts = []
    for d in range(1, n_face):
        parts.append(
            pltpu.make_async_remote_copy(
                src_ref=part.at[face],
                dst_ref=part.at[face],
                send_sem=part_send.at[d],
                recv_sem=part_recv.at[d],
                device_id=(lax.rem(face + d, n_face), sub),
                device_id_type=MESH,
            )
        )
    for copy in parts:
        copy.start()

    def remote(src, src_at, rows, to, peer, i):
        return pltpu.make_async_remote_copy(
            src_ref=src.at[pl.ds(src_at, rows)],
            dst_ref=xe.at[pl.ds(to, rows)],
            send_sem=halo_send.at[i],
            recv_sem=halo_recv.at[i],
            device_id=peer,
            device_id_type=MESH,
        )

    bottom = 3 * EXT_ROW
    last = ROW - BT
    edges = [
        remote(x_ref, 0, BT, bottom + BT, (up, sub), 0),
        remote(x_ref, ROW, BT, BT, (down, sub), 1),
        remote(x_ref, last, BT, bottom + BC * BT, (up, sub), 2),
        remote(x_ref, ROW + last, BT, BC * BT, (down, sub), 3),
    ]

    def chunk(k):
        at = BT + k * (2 * BT)
        return [
            remote(x_ref, at, 2 * BT, bottom + BT + at, (up, sub), 4 + 2 * k),
            remote(x_ref, ROW + at, 2 * BT, BT + at, (down, sub), 5 + 2 * k),
        ]

    sides = [
        remote(x_ref, last, BT, EXT_ROW, (face, right), 10),
        remote(x_ref, ROW + last, BT, 2 * EXT_ROW, (face, right), 11),
        remote(x_ref, 0, BT, EXT_ROW + 9 * BT, (face, left), 12),
        remote(x_ref, ROW, BT, 2 * EXT_ROW + 9 * BT, (face, left), 13),
    ]
    corners = [
        remote(xe, BC * BT, BT, 0, (face, right), 14),
        remote(xe, bottom + BC * BT, BT, bottom, (face, right), 15),
        remote(xe, BT, BT, 9 * BT, (face, left), 16),
        remote(xe, bottom + BT, BT, bottom + 9 * BT, (face, left), 17),
    ]
    for copy in edges + chunk(0):
        copy.start()

    lax.fori_loop(0, 2, matmul(own_at, ROW, 2 * D, kv, own_at, D, 512, None), 0)

    for copy in parts:
        copy.wait()
    for k in range(n_face // 2):
        cells[slot, pl.ds(2 * k, 2), :] = part[2 * k] + part[2 * k + 1]

    def gather(at, count, peer, i):
        return pltpu.make_async_remote_copy(
            src_ref=cells.at[pl.ds(at, count)],
            dst_ref=cells.at[pl.ds(at, count)],
            send_sem=cell_send.at[i],
            recv_sem=cell_recv.at[i],
            device_id=(face, peer),
            device_id_type=MESH,
        )

    gather_z = gather(slot, 1, across, 0)
    gather_y = [gather(shelf, 2, peer, 1 + i) for i, peer in enumerate(along)]
    gather_core = gather(core * (2 * n_y), 2 * n_y, mate, n_y)
    gather_z.start()
    gather_z.wait()
    for copy in gather_y:
        copy.start()
    for copy in chunk(1):
        copy.start()

    def project(starts):
        lax.fori_loop(0, 2, matmul(starts, BT, D, kv, starts, 0, D, None), 0)

    for copy in edges:
        copy.wait_recv()
    for copy in corners:
        copy.start()
    project([BT, BC * BT, bottom + BT, bottom + BC * BT])

    for copy in gather_y:
        copy.wait()
    gather_core.start()
    for copy in chunk(2):
        copy.start()
    gather_core.wait()
    for copy in sides:
        copy.start()

    one = cells[...].reshape(n_one, D)
    one_hi = one.astype(BF)
    one_lo = (one - one_hi.astype(F32)).astype(BF)
    pick = (
        lax.broadcasted_iota(jnp.int32, (n_two, n_one), 1) // 4
        == lax.broadcasted_iota(jnp.int32, (n_two, n_one), 0)
    ).astype(BF)
    two = jnp.dot(pick, one_hi, preferred_element_type=F32) + jnp.dot(
        pick, one_lo, preferred_element_type=F32
    )
    two_hi = two.astype(BF)
    two_lo = (two - two_hi.astype(F32)).astype(BF)
    sums = jnp.concatenate([one_hi, two_hi, one_lo, two_lo], axis=0)
    same = (
        lax.broadcasted_iota(jnp.int32, (GW, GW), 0) // HD
        == lax.broadcasted_iota(jnp.int32, (GW, GW), 1) // HD
    )
    mean = jnp.where(same, 1.0 / HD, 0.0).astype(BF)

    def pooled(n, carry):
        cols = pl.ds(pl.multiple_of(n * GW, GW), GW)
        wcols = pl.ds(pl.multiple_of(D + n * GW, GW), GW)
        y = jnp.dot(sums, wq[:, wcols], preferred_element_type=F32)
        y = y[:n_far] + y[n_far:]
        sq = jnp.dot((y * y).astype(BF), mean, preferred_element_type=F32)
        far[:, cols] = (y * lax.rsqrt(sq + 1e-5)).astype(BF)
        return carry

    lax.fori_loop(0, 2 * D // GW, pooled, 0)

    lane = lax.broadcasted_iota(jnp.int32, (BT, GW), 1) // HD
    lane_far = lax.broadcasted_iota(jnp.int32, (BT, 128), 1)

    def attend(c):
        items = []
        for r in range(BR):
            corner = r * EXT_ROW + c * BT
            me = corner + EXT_ROW + BT
            b = r * BC + c
            own_id = near_ref[b, 4]
            starts = []
            for j in range(9):
                at = corner + j // 3 * EXT_ROW + j % 3 * BT
                if j in (0, 2, 6, 8):
                    other = near_ref[b, j] - own_id
                    at = me + (at - me) * jnp.minimum(other * other, 1)
                starts.append(at)
            rows = pl.ds(pl.multiple_of(b * BT, BT), BT)
            items += [(rows, starts, g) for g in range(HEADS // GROUP)]

        def scores(rows, starts, g):
            cols = pl.ds(g * GW, GW)
            qb = q[rows, cols]
            zero = jnp.zeros_like(qb)
            qs = jnp.concatenate([jnp.where(lane == h, qb, zero) for h in range(GROUP)], axis=0)
            keys = jnp.concatenate(
                [far[:, cols]] + [kv[pl.ds(at, BT), cols] for at in starts], axis=0
            )
            return lax.dot_general(
                qs, keys, (((1,), (1,)), ((), ())), preferred_element_type=F32
            )

        s_next = scores(*items[0])
        for i, (rows, starts, g) in enumerate(items):
            s = s_next
            if i + 1 < len(items):
                s_next = scores(*items[i + 1])
            add_one = jnp.concatenate(
                [jnp.full((BT, 128), bias_ref[0, g * GROUP + h] * LOG2E, F32) for h in range(GROUP)],
                axis=0,
            )
            add_two = jnp.concatenate(
                [
                    jnp.where(lane_far < n_two, bias_ref[1, g * GROUP + h] * LOG2E, 0.0)
                    for h in range(GROUP)
                ],
                axis=0,
            )
            s = jnp.concatenate(
                [s[:, :128] + add_one, s[:, 128:256] + add_two, s[:, 256:]], axis=1
            )
            p = jnp.exp2(s - jnp.max(s, axis=1, keepdims=True))
            total = jnp.sum(p, axis=1, keepdims=True)
            vcols = pl.ds(D + g * GW, GW)
            vals = jnp.concatenate(
                [far[:, vcols]] + [kv[pl.ds(at, BT), vcols] for at in starts], axis=0
            )
            o = jnp.dot(p.astype(BF), vals, preferred_element_type=F32)
            o = o * (1.0 / total)
            h01 = jnp.where(lane == 0, o[:BT], o[BT : 2 * BT])
            h23 = jnp.where(lane == 2, o[2 * BT : 3 * BT], o[3 * BT :])
            heard[rows, pl.ds(g * GW, GW)] = jnp.where(lane < 2, h01, h23).astype(BF)

    def middle(k, carry):
        for copy in chunk(k):
            copy.wait_recv()
        at = 2 * BT + k * (2 * BT)
        project([at, at + BT, bottom + at, bottom + at + BT])

        def column(c, carry):
            attend(c)
            return carry

        lax.fori_loop(1 + k * (k + 1) // 2, 1 + (k + 1) * (k + 2) // 2, column, 0)
        return carry

    lax.fori_loop(0, 3, middle, 0)

    for copy in sides + corners:
        copy.wait_recv()

    def outer(i, carry):
        at = i * (9 * BT)
        project([at, EXT_ROW + at, 2 * EXT_ROW + at, bottom + at])
        attend(i * (BC - 1))
        return carry

    lax.fori_loop(0, 2, outer, 0)

    loads[5].wait()
    stores = []
    for i in range(BR):
        rows = pl.ds(i * ROW, ROW)
        y = jnp.dot(heard[rows, :], wo[...], preferred_element_type=F32)
        mixed[rows, :] = y.astype(BF)
        store = pltpu.make_async_copy(mixed.at[rows], out_ref.at[rows], store_sem.at[i])
        store.start()
        stores.append(store)
    for copy in edges + chunk(0) + chunk(1) + chunk(2) + sides + corners:
        copy.wait_send()
    for store in stores:
        store.wait()


def solution(mesh):
    n_face, n_sub = mesh.shape["face"], mesh.shape["sub"]
    tokens = BR * ROW
    n_far = n_sub * 10

    def body(x, w_qkv, w_out, neighbours, parent_one, parent_two, level_bias):
        call = pl.pallas_call(
            functools.partial(kernel, n_face, n_sub),
            out_shape=jax.ShapeDtypeStruct((tokens, D), BF),
            in_specs=[pl.BlockSpec(memory_space=pl.ANY)] * 3
            + [pl.BlockSpec(memory_space=pltpu.SMEM)] * 2,
            out_specs=pl.BlockSpec(memory_space=pl.ANY),
            scratch_shapes=[
                pltpu.VMEM((EXT, D), BF),
                pltpu.VMEM((D, 3 * D), BF),
                pltpu.VMEM((D, D), BF),
                pltpu.VMEM((tokens, D), BF),
                pltpu.VMEM((EXT, 2 * D), BF),
                pltpu.VMEM((tokens, D), BF),
                pltpu.VMEM((tokens, D), BF),
                pltpu.VMEM((n_face, 2, D), F32),
                pltpu.VMEM((n_sub, 8, D), F32),
                pltpu.VMEM((n_far, 2 * D), BF),
                pltpu.SemaphoreType.DMA((6,)),
                pltpu.SemaphoreType.DMA((BR,)),
                pltpu.SemaphoreType.DMA((18,)),
                pltpu.SemaphoreType.DMA((18,)),
                pltpu.SemaphoreType.DMA((n_face,)),
                pltpu.SemaphoreType.DMA((n_face,)),
                pltpu.SemaphoreType.DMA((n_sub,)),
                pltpu.SemaphoreType.DMA((n_sub,)),
            ],
            compiler_params=pltpu.CompilerParams(
                collective_id=0, has_side_effects=True, vmem_limit_bytes=56 * 1024 * 1024
            ),
            cost_estimate=pl.CostEstimate(
                flops=60_000_000_000, bytes_accessed=16_000_000, transcendentals=12_000_000
            ),
        )
        return call(x, w_qkv, w_out, neighbours, level_bias)

    placed = (
        P(("face", "sub"), None),
        P(),
        P(),
        P(("face", "sub"), None),
        P(("face", "sub")),
        P(),
        P(),
    )
    return jax.shard_map(
        body, mesh=mesh, in_specs=placed, out_specs=P(("face", "sub"), None), check_vma=False
    )
```

time: 102 us -> 75.2 us (0.74)
  Pallas kernels: 98.4 us -> 71.9 us
    pallas_call x1, Pallas kernels: 98.4 us -> 71.9 us  [body(): return call(x, w_qkv, w_out, neighbours, level_bias)]
where the time goes in v2:
time: 75.2 us; the launch traced here: 75 us
  Pallas kernels  71.9 us (96%)
  local copies, waits for them, and re-layouts  3.08 us (4%)
    pallas_call x1, Pallas kernels, body(): return call(x, w_qkv, w_out, neighbours, level_bias)  71.9 us
    unnamed x1, local copies, waits for them, and re-layouts  3.08 us

profile of v2, /device:TPU:1, one launch (start us, length us, event | category | flops | bytes accessed | tf_op | source)
XLA Modules:
  0.0 75.0 jit_solution(11122853722151308837)
XLA Ops:
  0.0 71.9 %shard_map.55 = bf16[1024,1024]{1,0:T(8,128)(2,1)} custom-call(bf16[1024,1024]{1,0:T(8,128)(2,1)} %x_ref.1, bf16[1024,3072]{1,0:T(8,128)(2,1)} %wqkv_ref.1, bf16[1024,1024]{1,0:T(8,128)(2,1)} %wout_ref.1, s32[16,9]{1,0:T(8,128)} %near_ref.1, f32[2,16]{1,0:T(2,128)} %bias_ref.1), custom_call_target="tpu_custom_call" | custom-call | flops 60000002048 | bytes 16000000 | tf_op jit(solution)/shard_map/pallas_call | solution.py:409
  71.9 3.1 %copy.7 = bf16[1024,1024]{1,0:T(8,128)(2,1)} copy(bf16[1024,1024]{1,0:T(8,128)(2,1)} %shard_map.55) | data formatting | bytes 4194304

commit v3 on v2

--- a/solution.py
+++ b/solution.py
@@ -70,9 +70,9 @@
     along = [lax.rem(sub + d, n_sub) for d in range(4, n_sub, 4)]
     n_y = n_sub // 4
     shelf = core * (2 * n_y) + sub // 4 * 2
-    slot = shelf + high
 
     peers = [(lax.rem(face + d, n_face), sub) for d in range(1, n_face)]
+    peers += [(lax.rem(face + d, n_face), across) for d in range(1, n_face)]
     peers += [(face, left), (face, right), (face, across)] + [(face, far_y) for far_y in along]
     barrier = pltpu.get_barrier_semaphore()
     for peer in peers:
@@ -103,7 +103,7 @@
             tok = xe[pl.ds(to + half * (ROW // 2), ROW // 2), :].astype(F32)
             s = jnp.sum(tok, axis=0, keepdims=True)
             total = s if total is None else total + s
-        part[face, pl.ds(half, 1), :] = total
+        part[high * n_face + face, pl.ds(half, 1), :] = total
 
     def matmul(row_starts, rows, first, out, out_starts, out_first, width, scale):
         def step(n, carry):
@@ -122,25 +122,17 @@
         return step
 
     own_at = [to for to, _ in own]
-    loads[2].wait()
-    lax.fori_loop(
-        0, 2, matmul(own_at, ROW, 0, q, [0, ROW], 0, 512, HD**-0.5 * LOG2E), 0
-    )
-    loads[3].wait()
-    lax.fori_loop(0, 2, matmul(own_at, ROW, D, kv, own_at, 0, 512, None), 0)
-    loads[4].wait()
-
     pl.semaphore_wait(barrier, len(peers))
 
     parts = []
-    for d in range(1, n_face):
+    for d in range(1, 2 * n_face):
         parts.append(
             pltpu.make_async_remote_copy(
-                src_ref=part.at[face],
-                dst_ref=part.at[face],
+                src_ref=part.at[high * n_face + face],
+                dst_ref=part.at[high * n_face + face],
                 send_sem=part_send.at[d],
                 recv_sem=part_recv.at[d],
-                device_id=(lax.rem(face + d, n_face), sub),
+                device_id=(lax.rem(face + d, n_face), sub if d < n_face else across),
                 device_id_type=MESH,
             )
         )
@@ -171,6 +163,13 @@
         return [
             remote(x_ref, at, 2 * BT, bottom + BT + at, (up, sub), 4 + 2 * k),
             remote(x_ref, ROW + at, 2 * BT, BT + at, (down, sub), 5 + 2 * k),
+        ]
+
+    def half(k, i):
+        at = BT + k * (2 * BT) + i * BT
+        return [
+            remote(x_ref, at, BT, bottom + BT + at, (up, sub), 4 + 2 * k),
+            remote(x_ref, ROW + at, BT, BT + at, (down, sub), 5 + 2 * k),
         ]
 
     sides = [
@@ -185,15 +184,22 @@
         remote(xe, BT, BT, 9 * BT, (face, left), 16),
         remote(xe, bottom + BT, BT, bottom + 9 * BT, (face, left), 17),
     ]
-    for copy in edges + chunk(0):
-        copy.start()
-
-    lax.fori_loop(0, 2, matmul(own_at, ROW, 2 * D, kv, own_at, D, 512, None), 0)
+    for copy in edges[:2]:
+        copy.start()
+
+    loads[2].wait()
+    lax.fori_loop(
+        0, 2, matmul(own_at, ROW, 0, q, [0, ROW], 0, 512, HD**-0.5 * LOG2E), 0
+    )
+    loads[3].wait()
+    lax.fori_loop(0, 2, matmul(own_at, ROW, D, kv, own_at, 0, 512, None), 0)
 
     for copy in parts:
         copy.wait()
-    for k in range(n_face // 2):
-        cells[slot, pl.ds(2 * k, 2), :] = part[2 * k] + part[2 * k + 1]
+    for h in range(2):
+        for k in range(n_face // 2):
+            pair = part[h * n_face + 2 * k] + part[h * n_face + 2 * k + 1]
+            cells[shelf + h, pl.ds(2 * k, 2), :] = pair
 
     def gather(at, count, peer, i):
         return pltpu.make_async_remote_copy(
@@ -205,15 +211,14 @@
             device_id_type=MESH,
         )
 
-    gather_z = gather(slot, 1, across, 0)
     gather_y = [gather(shelf, 2, peer, 1 + i) for i, peer in enumerate(along)]
     gather_core = gather(core * (2 * n_y), 2 * n_y, mate, n_y)
-    gather_z.start()
-    gather_z.wait()
     for copy in gather_y:
         copy.start()
-    for copy in chunk(1):
-        copy.start()
+    for copy in edges[2:]:
+        copy.start()
+    loads[4].wait()
+    lax.fori_loop(0, 2, matmul(own_at, ROW, 2 * D, kv, own_at, D, 512, None), 0)
 
     def project(starts):
         lax.fori_loop(0, 2, matmul(starts, BT, D, kv, starts, 0, D, None), 0)
@@ -227,10 +232,10 @@
     for copy in gather_y:
         copy.wait()
     gather_core.start()
-    for copy in chunk(2):
+    for copy in half(0, 0):
         copy.start()
     gather_core.wait()
-    for copy in sides:
+    for copy in half(0, 1) + chunk(1) + sides + chunk(2):
         copy.start()
 
     one = cells[...].reshape(n_one, D)
@@ -341,13 +346,14 @@
 
     lax.fori_loop(0, 3, middle, 0)
 
-    for copy in sides + corners:
-        copy.wait_recv()
-
     def outer(i, carry):
-        at = i * (9 * BT)
+        side = core + i - 2 * core * i
+        side = 1 - side
+        at = side * (9 * BT)
+        for row, sem in ((EXT_ROW, 10), (2 * EXT_ROW, 11), (0, 14), (bottom, 15)):
+            remote(x_ref, 0, BT, row + at, (face, left), sem + 2 * side).wait_recv()
         project([at, EXT_ROW + at, 2 * EXT_ROW + at, bottom + at])
-        attend(i * (BC - 1))
+        attend(side * (BC - 1))
         return carry
 
     lax.fori_loop(0, 2, outer, 0)
@@ -387,15 +393,15 @@
                 pltpu.VMEM((EXT, 2 * D), BF),
                 pltpu.VMEM((tokens, D), BF),
                 pltpu.VMEM((tokens, D), BF),
-                pltpu.VMEM((n_face, 2, D), F32),
+                pltpu.VMEM((2 * n_face, 2, D), F32),
                 pltpu.VMEM((n_sub, 8, D), F32),
                 pltpu.VMEM((n_far, 2 * D), BF),
                 pltpu.SemaphoreType.DMA((6,)),
                 pltpu.SemaphoreType.DMA((BR,)),
                 pltpu.SemaphoreType.DMA((18,)),
                 pltpu.SemaphoreType.DMA((18,)),
-                pltpu.SemaphoreType.DMA((n_face,)),
-                pltpu.SemaphoreType.DMA((n_face,)),
+                pltpu.SemaphoreType.DMA((2 * n_face,)),
+                pltpu.SemaphoreType.DMA((2 * n_face,)),
                 pltpu.SemaphoreType.DMA((n_sub,)),
                 pltpu.SemaphoreType.DMA((n_sub,)),
             ],

time: 75.2 us -> 68.7 us (0.914)
  Pallas kernels: 71.9 us -> 65.2 us
    pallas_call x1, Pallas kernels: 71.9 us -> 65.2 us  [body(): return call(x, w_qkv, w_out, neighbours, level_bias)]
where the time goes in v3:
time: 68.7 us; the launch traced here: 68.3 us
  Pallas kernels  65.2 us (95%)
  local copies, waits for them, and re-layouts  3.08 us (4%)
    pallas_call x1, Pallas kernels, body(): return call(x, w_qkv, w_out, neighbours, level_bias)  65.2 us
    unnamed x1, local copies, waits for them, and re-layouts  3.08 us

profile of v3, /device:TPU:1, one launch (start us, length us, event | category | flops | bytes accessed | tf_op | source)
XLA Modules:
  0.0 68.3 jit_solution(16002159570957163237)
XLA Ops:
  0.0 65.2 %shard_map.55 = bf16[1024,1024]{1,0:T(8,128)(2,1)} custom-call(bf16[1024,1024]{1,0:T(8,128)(2,1)} %x_ref.1, bf16[1024,3072]{1,0:T(8,128)(2,1)} %wqkv_ref.1, bf16[1024,1024]{1,0:T(8,128)(2,1)} %wout_ref.1, s32[16,9]{1,0:T(8,128)} %near_ref.1, f32[2,16]{1,0:T(2,128)} %bias_ref.1), custom_call_target="tpu_custom_call" | custom-call | flops 60000002048 | bytes 16000000 | tf_op jit(solution)/shard_map/pallas_call | solution.py:415
  65.2 3.1 %copy.7 = bf16[1024,1024]{1,0:T(8,128)(2,1)} copy(bf16[1024,1024]{1,0:T(8,128)(2,1)} %shard_map.55) | data formatting | bytes 4194304

commit v4 on v3

--- a/solution.py
+++ b/solution.py
@@ -30,17 +30,14 @@
     n_sub,
     x_ref,
     wqkv_ref,
-    wout_ref,
     near_ref,
     bias_ref,
     out_ref,
     xe,
     wq,
-    wo,
     q,
     kv,
     heard,
-    mixed,
     part,
     cells,
     far,
@@ -91,7 +88,6 @@
         loads.append(
             pltpu.make_async_copy(wqkv_ref.at[:, cols], wq.at[:, cols], load_sem.at[2 + i])
         )
-    loads.append(pltpu.make_async_copy(wout_ref, wo, load_sem.at[5]))
     for load in loads:
         load.start()
 
@@ -258,18 +254,25 @@
     mean = jnp.where(same, 1.0 / HD, 0.0).astype(BF)
 
     def pooled(n, carry):
-        cols = pl.ds(pl.multiple_of(n * GW, GW), GW)
-        wcols = pl.ds(pl.multiple_of(D + n * GW, GW), GW)
+        width = 2 * GW
+        wcols = pl.ds(pl.multiple_of(D + n * width, width), width)
         y = jnp.dot(sums, wq[:, wcols], preferred_element_type=F32)
         y = y[:n_far] + y[n_far:]
-        sq = jnp.dot((y * y).astype(BF), mean, preferred_element_type=F32)
-        far[:, cols] = (y * lax.rsqrt(sq + 1e-5)).astype(BF)
+        for i in range(2):
+            z = y[:, i * GW : (i + 1) * GW]
+            sq = jnp.dot((z * z).astype(BF), mean, preferred_element_type=F32)
+            cols = pl.ds(pl.multiple_of(n * width + i * GW, GW), GW)
+            far[:, cols] = (z * lax.rsqrt(sq + 1e-5)).astype(BF)
         return carry
 
-    lax.fori_loop(0, 2 * D // GW, pooled, 0)
+    lax.fori_loop(0, D // GW, pooled, 0)
 
     lane = lax.broadcasted_iota(jnp.int32, (BT, GW), 1) // HD
     lane_far = lax.broadcasted_iota(jnp.int32, (BT, 128), 1)
+
+    def store(b):
+        rows = pl.ds(pl.multiple_of(b * BT, BT), BT)
+        return pltpu.make_async_copy(heard.at[rows], out_ref.at[rows], store_sem.at[b])
 
     def attend(c):
         items = []
@@ -330,6 +333,8 @@
             h01 = jnp.where(lane == 0, o[:BT], o[BT : 2 * BT])
             h23 = jnp.where(lane == 2, o[2 * BT : 3 * BT], o[3 * BT :])
             heard[rows, pl.ds(g * GW, GW)] = jnp.where(lane < 2, h01, h23).astype(BF)
+        for r in range(BR):
+            store(r * BC + c).start()
 
     def middle(k, carry):
         for copy in chunk(k):
@@ -358,19 +363,14 @@
 
     lax.fori_loop(0, 2, outer, 0)
 
-    loads[5].wait()
-    stores = []
-    for i in range(BR):
-        rows = pl.ds(i * ROW, ROW)
-        y = jnp.dot(heard[rows, :], wo[...], preferred_element_type=F32)
-        mixed[rows, :] = y.astype(BF)
-        store = pltpu.make_async_copy(mixed.at[rows], out_ref.at[rows], store_sem.at[i])
-        store.start()
-        stores.append(store)
     for copy in edges + chunk(0) + chunk(1) + chunk(2) + sides + corners:
         copy.wait_send()
-    for store in stores:
-        store.wait()
+    for b in range(BR * BC):
+        store(b).wait()
+
+
+def out_kernel(heard_ref, w_ref, out_ref):
+    out_ref[...] = jnp.dot(heard_ref[...], w_ref[...], preferred_element_type=F32).astype(BF)
 
 
 def solution(mesh):
@@ -382,22 +382,20 @@
         call = pl.pallas_call(
             functools.partial(kernel, n_face, n_sub),
             out_shape=jax.ShapeDtypeStruct((tokens, D), BF),
-            in_specs=[pl.BlockSpec(memory_space=pl.ANY)] * 3
+            in_specs=[pl.BlockSpec(memory_space=pl.ANY)] * 2
             + [pl.BlockSpec(memory_space=pltpu.SMEM)] * 2,
             out_specs=pl.BlockSpec(memory_space=pl.ANY),
             scratch_shapes=[
                 pltpu.VMEM((EXT, D), BF),
                 pltpu.VMEM((D, 3 * D), BF),
-                pltpu.VMEM((D, D), BF),
                 pltpu.VMEM((tokens, D), BF),
                 pltpu.VMEM((EXT, 2 * D), BF),
-                pltpu.VMEM((tokens, D), BF),
                 pltpu.VMEM((tokens, D), BF),
                 pltpu.VMEM((2 * n_face, 2, D), F32),
                 pltpu.VMEM((n_sub, 8, D), F32),
                 pltpu.VMEM((n_far, 2 * D), BF),
-                pltpu.SemaphoreType.DMA((6,)),
-                pltpu.SemaphoreType.DMA((BR,)),
+                pltpu.SemaphoreType.DMA((5,)),
+                pltpu.SemaphoreType.DMA((BR * BC,)),
                 pltpu.SemaphoreType.DMA((18,)),
                 pltpu.SemaphoreType.DMA((18,)),
                 pltpu.SemaphoreType.DMA((2 * n_face,)),
@@ -412,7 +410,19 @@
                 flops=60_000_000_000, bytes_accessed=16_000_000, transcendentals=12_000_000
             ),
         )
-        return call(x, w_qkv, w_out, neighbours, level_bias)
+        heard = call(x, w_qkv, neighbours, level_bias)
+        rows = tokens // 4
+        return pl.pallas_call(
+            out_kernel,
+            grid=(4,),
+            out_shape=jax.ShapeDtypeStruct((tokens, D), BF),
+            in_specs=[
+                pl.BlockSpec((rows, D), lambda i: (i, 0)),
+                pl.BlockSpec((D, D), lambda i: (0, 0)),
+            ],
+            out_specs=pl.BlockSpec((rows, D), lambda i: (i, 0)),
+            compiler_params=pltpu.CompilerParams(vmem_limit_bytes=32 * 1024 * 1024),
+        )(heard, w_out)
 
     placed = (
         P(("face", "sub"), None),

time: 68.7 us -> 68.6 us (level)
  local copies, waits for them, and re-layouts: 3.08 us -> 1.59 us
  Pallas kernels: 65.2 us -> 66.6 us
    unnamed x1 -> x4, local copies, waits for them, and re-layouts: 3.08 us -> 1.59 us
    pallas_call x1 -> x2, Pallas kernels: 65.2 us -> 66.6 us  [the longest x1 62.8 us: body(): heard = call(x, w_qkv, neighbours, level_bias)]
where the time goes in v4:
time: 68.6 us; the launch traced here: 68.2 us
  Pallas kernels  66.6 us (97%)
  local copies, waits for them, and re-layouts  1.59 us (2%)
    pallas_call x1, Pallas kernels, body(): heard = call(x, w_qkv, neighbours, level_bias)  62.8 us
    pallas_call x1, Pallas kernels, body(): pl.pallas_call(out_kernel, grid=(4,), out_shape=jax.ShapeDtypeStruct((tok...  3.72 us
    unnamed x4, local copies, waits for them, and re-layouts  1.59 us

profile of v4, /device:TPU:1, one launch (start us, length us, event | category | flops | bytes accessed | tf_op | source)
XLA Modules:
  0.0 68.2 jit_solution(969236184619230313)
XLA Ops:
  0.0 0.0 copy-start
  0.0 62.8 %shard_map.55.heard_ref = bf16[1024,1024]{1,0:T(8,128)(2,1)} custom-call(bf16[1024,1024]{1,0:T(8,128)(2,1)} %x_ref.1, bf16[1024,3072]{1,0:T(8,128)(2,1)} %wqkv_ref.1, s32[16,9]{1,0:T(8,128)} %near_ref.1, f32[2,16]{1,0:T(2,128)} %bias_ref.1), custom_call_target="tpu_custom_call" | custom-call | flops 60000002048 | bytes 16000000 | tf_op jit(solution)/shard_map/pallas_call | solution.py:413
  62.8 0.0 copy-done
  62.8 0.0 copy-start.1
  62.9 1.6 %copy-done.1 = bf16[1024,1024]{1,0:T(8,128)(2,1)S(1)} copy-done((bf16[1024,1024]{1,0:T(8,128)(2,1)S(1)}, bf16[1024,1024]{1,0:T(8,128)(2,1)}, u32[]{:S(2)}) %copy-start.1) | copy-done | bytes 2097176
  64.4 3.7 %shard_map.56 = bf16[1024,1024]{1,0:T(8,128)(2,1)} custom-call(bf16[1024,1024]{1,0:T(8,128)(2,1)S(1)} %copy-done.1, bf16[1024,1024]{1,0:T(8,128)(2,1)S(1)} %copy-done), custom_call_target="tpu_custom_call" | custom-call | tf_op jit(solution)/shard_map/pallas_call | solution.py:415
Async XLA Ops:
  0.0 62.8 %copy-start = (bf16[1024,1024]{1,0:T(8,128)(2,1)S(1)}, bf16[1024,1024]{1,0:T(8,128)(2,1)}, u32[]{:S(2)}) copy-start(bf16[1024,1024]{1,0:T(8,128)(2,1)} %w_ref.1) | copy-start | bytes 6291460
  62.8 1.6 %copy-start.1 = (bf16[1024,1024]{1,0:T(8,128)(2,1)S(1)}, bf16[1024,1024]{1,0:T(8,128)(2,1)}, u32[]{:S(2)}) copy-start(bf16[1024,1024]{1,0:T(8,128)(2,1)} %shard_map.55.heard_ref) | copy-start | bytes 6291460
